TPU v7x, 32 devices: a whole 2x2x4 slice. The times are simulated.
32 devices in a mesh: clip: 1, head: 16 (over z, y, x), kv: 2 (over core).
Axes of the slice: x: 2, y: 2, z: 4, core: 2. Of those that a mesh axis runs over, the one named last changes fastest.
Arguments:
- queries: bfloat16 [4096, 4096], P(('clip', 'head')), may hold values from -7 to 7
- keys: bfloat16 [8192, 4096], P(('clip', 'head', 'kv')), may hold values from -5 to 5
- values: bfloat16 [8192, 4096], P(('clip', 'head', 'kv')), may hold values from -6 to 6
- tile_list: int32 [32, 32], P('clip'), may hold values from 0 to 63, as said below
Outputs:
- attended: bfloat16 [4096, 4096], P(('clip', 'head', 'kv'))
Inputs may be any that keep to these rules, and one draw needn't show every extreme that they name: `tile_list`: each row names 32 different key tiles. Calling a tile t even when (t // 2) is even, a row names at most 20 even tiles and at most 20 others; some row names exactly 20 even tiles and some row exactly 20 others, in every draw.
All inputs are finite; a program needn't handle non-finite values.
Results may differ from a plain program's by a relative error of at most 0.014.
Values may be sent and summed in bfloat16 or wider, within the bound.
A program may use at most 128 MiB of HBM per device.

v0:
```python
import math

import jax
import jax.numpy as jnp
from jax import lax
from jax.sharding import PartitionSpec as P

HEADS = 32
DH = 128
TILE = 128
KTOK_DEV = 256


def local(queries, keys, values, tile_list):
    n_head = lax.axis_size("head")
    heads_dev = HEADS // n_head
    kv_index = lax.axis_index("kv")
    key_all, value_all = (
        lax.all_to_all(keys, "head", split_axis=1, concat_axis=0, tiled=True),
        lax.all_to_all(values, "head", split_axis=1, concat_axis=0, tiled=True),
    )
    tile_span = KTOK_DEV // TILE
    key_shard = tile_list // tile_span
    parity = key_shard % 2
    local_tile = key_shard // 2 * tile_span + tile_list % tile_span
    inv_root = 1.0 / jnp.sqrt(jnp.float32(DH))
    feat_width = key_all.shape[1]
    half_rows = queries.shape[0] // 2
    own_rows = lax.dynamic_slice_in_dim(queries, kv_index * half_rows, half_rows, 0)
    query_part = lax.all_to_all(own_rows, "head", split_axis=1, concat_axis=0, tiled=True)
    key_source, value_source = (
        lax.all_gather(key_all, "kv", axis=0, tiled=True),
        lax.all_gather(value_all, "kv", axis=0, tiled=True),
    )
    full_tile = parity * (key_all.shape[0] // TILE) + local_tile
    unit_rows = min(half_rows, TILE)
    unit_count = query_part.shape[0] // unit_rows
    unit_pos = jnp.arange(unit_count, dtype=jnp.int32) * unit_rows
    source_head = unit_pos // half_rows
    first_row = source_head * (2 * half_rows) + kv_index * half_rows + unit_pos % half_rows
    unit_tile = first_row // TILE
    query_tile_ids = jnp.arange(tile_list.shape[0], dtype=jnp.int32)
    onehot = (unit_tile[:, None] == query_tile_ids[None, :]).astype(jnp.int32)
    unit_lists = jnp.sum(onehot[:, :, None] * full_tile[None, :, :], axis=1)
    block_units = math.gcd(unit_count, max(1, 512 // unit_rows))
    key_tiles = key_source.reshape(-1, TILE, feat_width)
    value_tiles = value_source.reshape(-1, TILE, feat_width)
    slot_count = unit_lists.shape[1]

    def unit_block(block_index):
        query_block = lax.dynamic_slice_in_dim(
            query_part, block_index * block_units * unit_rows, block_units * unit_rows, 0
        )
        query_block = query_block.reshape(block_units, unit_rows, heads_dev, DH)
        tile_ids = lax.dynamic_slice_in_dim(unit_lists, block_index * block_units, block_units, 0)
        key_block = key_tiles[tile_ids].reshape(block_units, slot_count * TILE, heads_dev, DH)
        value_block = value_tiles[tile_ids].reshape(block_units, slot_count * TILE, heads_dev, DH)
        scores = (
            jnp.einsum(
                "bqhd,bkhd->bhqk", query_block, key_block, preferred_element_type=jnp.float32
            )
            * inv_root
        )
        row_peak = jnp.max(scores, axis=-1)
        exponent = jnp.exp(scores - row_peak[..., None])
        row_total = jnp.sum(exponent, axis=-1)
        weight = exponent.astype(jnp.bfloat16)
        weighted = jnp.einsum(
            "bhqk,bkhd->bqhd", weight, value_block, preferred_element_type=jnp.float32
        )
        result = weighted / jnp.transpose(row_total, (0, 2, 1))[..., None]
        return result.astype(jnp.bfloat16).reshape(block_units * unit_rows, feat_width)

    block_rows = lax.map(unit_block, jnp.arange(unit_count // block_units, dtype=jnp.int32))
    normalized = block_rows.reshape(n_head, -1, feat_width)
    regrouped = lax.all_to_all(normalized, "head", split_axis=0, concat_axis=2, tiled=True)
    return regrouped.reshape(-1, HEADS * DH)


def solution(mesh):
    return jax.shard_map(
        local,
        mesh=mesh,
        in_specs=(
            P(("clip", "head"), None),
            P(("clip", "head", "kv"), None),
            P(("clip", "head", "kv"), None),
            P("clip", None),
        ),
        out_specs=P(("clip", "head", "kv"), None),
        check_vma=False,
    )
```

profile of v0, /device:TPU:0, one launch (start us, length us, event | category | flops | bytes accessed | tf_op | source)
XLA Modules:
  0.0 509.7 jit_solution(12329036469467087044)
XLA Ops:
  6.5 4.2 copy.49
  10.7 3.9 copy.50
  14.6 57.3 %all_to_all.72 = bf16[256,16,256]{2,0,1:T(8,128)(2,1)} all-to-all(bf16[256,16,256]{2,0,1:T(8,128)(2,1)} %copy.50), channel_id=1, replica_groups=mesh['clip'=1,'head'=16,'kv'=2] {'head'}, dimensions={1} | all-to-all | bytes 4194304 | tf_op jit(solution)/shard_map/all_to_all | solution.py:20
  72.0 4.1 copy.53
  76.1 4.1 copy.54
  80.2 51.9 %all_to_all.73 = bf16[256,16,256]{2,0,1:T(8,128)(2,1)} all-to-all(bf16[256,16,256]{2,0,1:T(8,128)(2,1)} %copy.54), channel_id=1, replica_groups=mesh['clip'=1,'head'=16,'kv'=2] {'head'}, dimensions={1} | all-to-all | bytes 4194304 | tf_op jit(solution)/shard_map/all_to_all | solution.py:19
  132.1 0.1 constant_dynamic-slice_fusion.1
  132.2 1.3 copy.57
  133.5 3.9 all-to-all-start.1
  137.6 0.1 multiply_reduce_fusion.1
  137.7 22.7 %all-to-all-done.1 = bf16[128,16,256]{0,2,1:T(8,128)(2,1)S(1)} async-done(((bf16[128,16,256]{0,2,1:T(8,128)(2,1)}), bf16[128,16,256]{0,2,1:T(8,128)(2,1)S(1)}, u32[]{:S(2)}, u32[]{:S(2)}) %all-to-all-start.1) | async-done | bytes 1048608 | tf_op jit(solution)/shard_map/all_to_all | solution.py:30
  160.5 0.5 copy.52
  161.1 307.2 %while.12 = (s32[]{:T(128)}, bf16[4,512,256]{2,1,0:T(8,128)(2,1)}, s32[4]{0:T(128)S(1)}, s32[16,32]{1,0:T(8,128)S(1)}, bf16[64,128,256]{2,1,0:T(8,128)(2,1)}, /*...) while((s32[]{:T(128)}, bf16[4,512,256]{2,1,0:T(8,128)(2,1)}, ...), condition=%wide.region_4.5_spmd, body=%wide.region_1.4_spmd.sunk | while | flops 2181299712 | bytes 137391856 | solution.py:74
  161.3 0.7 dynamic_slice.31
  162.6 0.1 reshape.156
  162.7 8.7 %gather_fusion = bf16[128,128,256]{2,1,0:T(8,128)(2,1)} fusion(bf16[64,128,256]{2,1,0:T(8,128)(2,1)} %get-tuple-element.190, s32[1024]{0:T(1024)S(1)} %pad_clamp_fusion.2), kind=kCustom, calls=%fused_computation.1.clone.1 | custom fusion | bytes 16777728 | tf_op jit(solution)/shard_map/while/body/eval_jaxpr/gather | solution.py:56
  171.5 12.6 %reshape.157 = bf16[4,4096,2,128]{3,2,1,0:T(2,128)(2,1)} reshape(bf16[128,128,256]{2,1,0:T(8,128)(2,1)} %gather_fusion) | data formatting | bytes 16777216 | tf_op jit(solution)/shard_map/while/body/eval_jaxpr/reshape | solution.py:56
  184.8 11.5 %multiply_reduce_fusion.3 = (f32[4,2,128]{2,1,0:T(2,128)S(1)}, f32[4,2,128,4096]{3,2,1,0:T(8,128)}) fusion(bf16[4,4096,2,128]{3,2,1,0:T(2,128)(2,1)} %reshape.157, bf16[4,128,2,128]{3,2,1,0:T(2,128)(2,1)S(1)} %reshape.158), kind=kOutput, calls=%fused_computation.3.clone.1 | convolution fusion | flops 1082129408 | bytes 25432064 | tf_op jit(solution)/shard_map/while/body/eval_jaxpr/bqhd,bkhd->bhqk/dot_general | solution.py:59
  196.3 8.7 %gather_fusion.1 = bf16[128,128,256]{2,1,0:T(8,128)(2,1)} fusion(bf16[64,128,256]{2,1,0:T(8,128)(2,1)} %get-tuple-element.188, s32[1024]{0:T(1024)S(1)} %pad_clamp_fusion.2), kind=kCustom, calls=%fused_computation.clone.1 | custom fusion | bytes 16777728 | tf_op jit(solution)/shard_map/while/body/eval_jaxpr/gather | solution.py:57
  205.0 12.6 %reshape.159 = bf16[4,4096,2,128]{3,2,1,0:T(2,128)(2,1)} reshape(bf16[128,128,256]{2,1,0:T(8,128)(2,1)} %gather_fusion.1) | data formatting | bytes 16777216 | tf_op jit(solution)/shard_map/while/body/eval_jaxpr/reshape | solution.py:57
  217.6 8.6 %fusion.44 = f32[4,2,128]{2,1,0:T(2,128)S(1)} fusion(f32[4,2,128,4096]{3,2,1,0:T(8,128)} %get-tuple-element.156, f32[4,2,128]{2,1,0:T(2,128)S(1)} %get-tuple-element.157), kind=kLoop, calls=%fused_computation.4.clone.1 | loop fusion | flops 12581888 | bytes 16785408 | tf_op jit(solution)/shard_map/while/body/eval_jaxpr/reduce_sum | solution.py:66
  226.2 10.8 %fusion.45 = bf16[4,128,2,128]{1,3,2,0:T(8,128)(2,1)S(1)} fusion(f32[4,2,128,4096]{3,2,1,0:T(8,128)} %get-tuple-element.156, f32[4,2,128]{2,1,0:T(2,128)S(1)} %get-tuple-element.157, bf16[4,4096,2,128]{3,2,1,0:T(2,128)(2,1)} %reshape.159, f32[4,128,2]{1,2,0:T(2,128)S(1)} %bitcast.45), kind=kOutput, calls=%fused_computation.14.clone.1 | convolution fusion | flops 1086586880 | bytes 25436160 | tf_op jit(solution)/shard_map/while/body/eval_jaxpr/bhqk,bkhd->bqhd/dot_general | solution.py:68
  237.0 0.2 copy.81
  237.2 0.2 broadcast_in_dim.25
  237.3 0.7 constant_dynamic-update-slice_fusion.2
  238.1 0.6 dynamic_slice.31
  239.4 0.1 reshape.156
  239.5 8.7 %gather_fusion = bf16[128,128,256]{2,1,0:T(8,128)(2,1)} fusion(bf16[64,128,256]{2,1,0:T(8,128)(2,1)} %get-tuple-element.190, s32[1024]{0:T(1024)S(1)} %pad_clamp_fusion.2), kind=kCustom, calls=%fused_computation.1.clone.1 | custom fusion | bytes 16777728 | tf_op jit(solution)/shard_map/while/body/eval_jaxpr/gather | solution.py:56
  248.3 12.6 %reshape.157 = bf16[4,4096,2,128]{3,2,1,0:T(2,128)(2,1)} reshape(bf16[128,128,256]{2,1,0:T(8,128)(2,1)} %gather_fusion) | data formatting | bytes 16777216 | tf_op jit(solution)/shard_map/while/body/eval_jaxpr/reshape | solution.py:56
  261.6 11.5 %multiply_reduce_fusion.3 = (f32[4,2,128]{2,1,0:T(2,128)S(1)}, f32[4,2,128,4096]{3,2,1,0:T(8,128)}) fusion(bf16[4,4096,2,128]{3,2,1,0:T(2,128)(2,1)} %reshape.157, bf16[4,128,2,128]{3,2,1,0:T(2,128)(2,1)S(1)} %reshape.158), kind=kOutput, calls=%fused_computation.3.clone.1 | convolution fusion | flops 1082129408 | bytes 25432064 | tf_op jit(solution)/shard_map/while/body/eval_jaxpr/bqhd,bkhd->bhqk/dot_general | solution.py:59
  273.1 8.7 %gather_fusion.1 = bf16[128,128,256]{2,1,0:T(8,128)(2,1)} fusion(bf16[64,128,256]{2,1,0:T(8,128)(2,1)} %get-tuple-element.188, s32[1024]{0:T(1024)S(1)} %pad_clamp_fusion.2), kind=kCustom, calls=%fused_computation.clone.1 | custom fusion | bytes 16777728 | tf_op jit(solution)/shard_map/while/body/eval_jaxpr/gather | solution.py:57
  281.8 12.6 %reshape.159 = bf16[4,4096,2,128]{3,2,1,0:T(2,128)(2,1)} reshape(bf16[128,128,256]{2,1,0:T(8,128)(2,1)} %gather_fusion.1) | data formatting | bytes 16777216 | tf_op jit(solution)/shard_map/while/body/eval_jaxpr/reshape | solution.py:57
  294.4 8.6 %fusion.44 = f32[4,2,128]{2,1,0:T(2,128)S(1)} fusion(f32[4,2,128,4096]{3,2,1,0:T(8,128)} %get-tuple-element.156, f32[4,2,128]{2,1,0:T(2,128)S(1)} %get-tuple-element.157), kind=kLoop, calls=%fused_computation.4.clone.1 | loop fusion | flops 12581888 | bytes 16785408 | tf_op jit(solution)/shard_map/while/body/eval_jaxpr/reduce_sum | solution.py:66
  303.0 10.8 %fusion.45 = bf16[4,128,2,128]{1,3,2,0:T(8,128)(2,1)S(1)} fusion(f32[4,2,128,4096]{3,2,1,0:T(8,128)} %get-tuple-element.156, f32[4,2,128]{2,1,0:T(2,128)S(1)} %get-tuple-element.157, bf16[4,4096,2,128]{3,2,1,0:T(2,128)(2,1)} %reshape.159, f32[4,128,2]{1,2,0:T(2,128)S(1)} %bitcast.45), kind=kOutput, calls=%fused_computation.14.clone.1 | convolution fusion | flops 1086586880 | bytes 25436160 | tf_op jit(solution)/shard_map/while/body/eval_jaxpr/bhqk,bkhd->bqhd/dot_general | solution.py:68
  313.7 0.2 copy.81
  313.9 0.2 broadcast_in_dim.25
  314.1 0.7 constant_dynamic-update-slice_fusion.2
  314.8 0.6 dynamic_slice.31
  316.2 0.1 reshape.156
  316.3 8.7 %gather_fusion = bf16[128,128,256]{2,1,0:T(8,128)(2,1)} fusion(bf16[64,128,256]{2,1,0:T(8,128)(2,1)} %get-tuple-element.190, s32[1024]{0:T(1024)S(1)} %pad_clamp_fusion.2), kind=kCustom, calls=%fused_computation.1.clone.1 | custom fusion | bytes 16777728 | tf_op jit(solution)/shard_map/while/body/eval_jaxpr/gather | solution.py:56
  325.0 12.6 %reshape.157 = bf16[4,4096,2,128]{3,2,1,0:T(2,128)(2,1)} reshape(bf16[128,128,256]{2,1,0:T(8,128)(2,1)} %gather_fusion) | data formatting | bytes 16777216 | tf_op jit(solution)/shard_map/while/body/eval_jaxpr/reshape | solution.py:56
  338.4 11.5 %multiply_reduce_fusion.3 = (f32[4,2,128]{2,1,0:T(2,128)S(1)}, f32[4,2,128,4096]{3,2,1,0:T(8,128)}) fusion(bf16[4,4096,2,128]{3,2,1,0:T(2,128)(2,1)} %reshape.157, bf16[4,128,2,128]{3,2,1,0:T(2,128)(2,1)S(1)} %reshape.158), kind=kOutput, calls=%fused_computation.3.clone.1 | convolution fusion | flops 1082129408 | bytes 25432064 | tf_op jit(solution)/shard_map/while/body/eval_jaxpr/bqhd,bkhd->bhqk/dot_general | solution.py:59
  349.8 8.7 %gather_fusion.1 = bf16[128,128,256]{2,1,0:T(8,128)(2,1)} fusion(bf16[64,128,256]{2,1,0:T(8,128)(2,1)} %get-tuple-element.188, s32[1024]{0:T(1024)S(1)} %pad_clamp_fusion.2), kind=kCustom, calls=%fused_computation.clone.1 | custom fusion | bytes 16777728 | tf_op jit(solution)/shard_map/while/body/eval_jaxpr/gather | solution.py:57
  358.6 12.6 %reshape.159 = bf16[4,4096,2,128]{3,2,1,0:T(2,128)(2,1)} reshape(bf16[128,128,256]{2,1,0:T(8,128)(2,1)} %gather_fusion.1) | data formatting | bytes 16777216 | tf_op jit(solution)/shard_map/while/body/eval_jaxpr/reshape | solution.py:57
  371.1 8.6 %fusion.44 = f32[4,2,128]{2,1,0:T(2,128)S(1)} fusion(f32[4,2,128,4096]{3,2,1,0:T(8,128)} %get-tuple-element.156, f32[4,2,128]{2,1,0:T(2,128)S(1)} %get-tuple-element.157), kind=kLoop, calls=%fused_computation.4.clone.1 | loop fusion | flops 12581888 | bytes 16785408 | tf_op jit(solution)/shard_map/while/body/eval_jaxpr/reduce_sum | solution.py:66
  379.7 10.8 %fusion.45 = bf16[4,128,2,128]{1,3,2,0:T(8,128)(2,1)S(1)} fusion(f32[4,2,128,4096]{3,2,1,0:T(8,128)} %get-tuple-element.156, f32[4,2,128]{2,1,0:T(2,128)S(1)} %get-tuple-element.157, bf16[4,4096,2,128]{3,2,1,0:T(2,128)(2,1)} %reshape.159, f32[4,128,2]{1,2,0:T(2,128)S(1)} %bitcast.45), kind=kOutput, calls=%fused_computation.14.clone.1 | convolution fusion | flops 1086586880 | bytes 25436160 | tf_op jit(solution)/shard_map/while/body/eval_jaxpr/bhqk,bkhd->bqhd/dot_general | solution.py:68
  390.5 0.2 copy.81
  390.7 0.2 broadcast_in_dim.25
  390.9 0.7 constant_dynamic-update-slice_fusion.2
  391.6 0.6 dynamic_slice.31
  392.9 0.1 reshape.156
  393.0 8.7 %gather_fusion = bf16[128,128,256]{2,1,0:T(8,128)(2,1)} fusion(bf16[64,128,256]{2,1,0:T(8,128)(2,1)} %get-tuple-element.190, s32[1024]{0:T(1024)S(1)} %pad_clamp_fusion.2), kind=kCustom, calls=%fused_computation.1.clone.1 | custom fusion | bytes 16777728 | tf_op jit(solution)/shard_map/while/body/eval_jaxpr/gather | solution.py:56
  401.8 12.6 %reshape.157 = bf16[4,4096,2,128]{3,2,1,0:T(2,128)(2,1)} reshape(bf16[128,128,256]{2,1,0:T(8,128)(2,1)} %gather_fusion) | data formatting | bytes 16777216 | tf_op jit(solution)/shard_map/while/body/eval_jaxpr/reshape | solution.py:56
  415.1 11.5 %multiply_reduce_fusion.3 = (f32[4,2,128]{2,1,0:T(2,128)S(1)}, f32[4,2,128,4096]{3,2,1,0:T(8,128)}) fusion(bf16[4,4096,2,128]{3,2,1,0:T(2,128)(2,1)} %reshape.157, bf16[4,128,2,128]{3,2,1,0:T(2,128)(2,1)S(1)} %reshape.158), kind=kOutput, calls=%fused_computation.3.clone.1 | convolution fusion | flops 1082129408 | bytes 25432064 | tf_op jit(solution)/shard_map/while/body/eval_jaxpr/bqhd,bkhd->bhqk/dot_general | solution.py:59
  426.6 8.7 %gather_fusion.1 = bf16[128,128,256]{2,1,0:T(8,128)(2,1)} fusion(bf16[64,128,256]{2,1,0:T(8,128)(2,1)} %get-tuple-element.188, s32[1024]{0:T(1024)S(1)} %pad_clamp_fusion.2), kind=kCustom, calls=%fused_computation.clone.1 | custom fusion | bytes 16777728 | tf_op jit(solution)/shard_map/while/body/eval_jaxpr/gather | solution.py:57
  435.3 12.6 %reshape.159 = bf16[4,4096,2,128]{3,2,1,0:T(2,128)(2,1)} reshape(bf16[128,128,256]{2,1,0:T(8,128)(2,1)} %gather_fusion.1) | data formatting | bytes 16777216 | tf_op jit(solution)/shard_map/while/body/eval_jaxpr/reshape | solution.py:57
  447.9 8.6 %fusion.44 = f32[4,2,128]{2,1,0:T(2,128)S(1)} fusion(f32[4,2,128,4096]{3,2,1,0:T(8,128)} %get-tuple-element.156, f32[4,2,128]{2,1,0:T(2,128)S(1)} %get-tuple-element.157), kind=kLoop, calls=%fused_computation.4.clone.1 | loop fusion | flops 12581888 | bytes 16785408 | tf_op jit(solution)/shard_map/while/body/eval_jaxpr/reduce_sum | solution.py:66
  456.5 10.8 %fusion.45 = bf16[4,128,2,128]{1,3,2,0:T(8,128)(2,1)S(1)} fusion(f32[4,2,128,4096]{3,2,1,0:T(8,128)} %get-tuple-element.156, f32[4,2,128]{2,1,0:T(2,128)S(1)} %get-tuple-element.157, bf16[4,4096,2,128]{3,2,1,0:T(2,128)(2,1)} %reshape.159, f32[4,128,2]{1,2,0:T(2,128)S(1)} %bitcast.45), kind=kOutput, calls=%fused_computation.14.clone.1 | convolution fusion | flops 1086586880 | bytes 25436160 | tf_op jit(solution)/shard_map/while/body/eval_jaxpr/bhqk,bkhd->bqhd/dot_general | solution.py:68
  467.2 0.2 copy.81
  467.4 0.2 broadcast_in_dim.25
  467.6 0.7 constant_dynamic-update-slice_fusion.2
  468.3 31.0 %all_to_all.74 = bf16[16,128,256]{2,1,0:T(8,128)(2,1)S(1)} all-to-all(bf16[16,128,256]{2,1,0:T(8,128)(2,1)} %bitcast.15), channel_id=1, replica_groups=mesh['clip'=1,'head'=16,'kv'=2] {'head'}, dimensions={0} | all-to-all | bytes 2097152 | tf_op jit(solution)/shard_map/all_to_all | solution.py:76
  499.3 1.3 copy.55
  500.6 2.3 copy.56
  (33 shorter events, 0.7 us)
Async XLA Ops:
  6.5 125.6 %copy-start = (bf16[256,4096]{1,0:T(8,128)(2,1)S(1)}, bf16[256,4096]{1,0:T(8,128)(2,1)}, u32[]{:S(2)}) copy-start(bf16[256,4096]{1,0:T(8,128)(2,1)} %param.6) | copy-start | bytes 6291460
  6.5 154.5 %all-gather.3.cloned.1.call-start = ((), (), s32[]{:S(2)}) async-start(), calls=%async_computation.4 | async-start | bytes 6291456 | tf_op jit(solution)/shard_map/all_gather | solution.py:33
  71.9 89.1 %all-gather.5.cloned.1.call-start = ((), (), s32[]{:S(2)}) async-start(), calls=%async_computation.5 | async-start | bytes 6291456 | tf_op jit(solution)/shard_map/all_gather | solution.py:32
  76.1 61.5 %copy-start.2 = (s32[32,32]{1,0:T(8,128)S(1)}, s32[32,32]{1,0:T(8,128)}, u32[]{:S(2)}) copy-start(s32[32,32]{1,0:T(8,128)} %param.9) | copy-start | bytes 12292
  133.5 26.9 %all-to-all-start.1 = ((bf16[128,16,256]{0,2,1:T(8,128)(2,1)}), bf16[128,16,256]{0,2,1:T(8,128)(2,1)S(1)}, u32[]{:S(2)}, u32[]{:S(2)}) async-start(bf16[128,16,256]{0,2,1:T(8,128)(2,1)} %bitcast.8), calls=%async_computation.1 | async-start | bytes 2097152 | tf_op jit(solution)/shard_map/all_to_all | solution.py:30
  468.3 34.6 %copy-start.1 = (bf16[256,4096]{1,0:T(8,128)(2,1)S(1)}, bf16[256,4096]{1,0:T(8,128)(2,1)}, u32[]{:S(2)}) copy-start(bf16[256,4096]{1,0:T(8,128)(2,1)} %param.6) | copy-start | bytes 6291460
Sparse Core Ops, SparseCore 0:
  72.0 11.9 all-gather.2
  132.2 11.9 all-gather.4
where the time goes:
time: 513 us; the launch traced here: 510 us
  local copies, waits for them, and re-layouts  200 us (39%)
  blocking collectives  140 us (27%)
  matrix products  88.9 us (17%)
  other arithmetic  34.8 us (7%)
  waiting for transfers between devices  22.8 us (4%)
  between operations  13.5 us (3%)
  loops' own time  5.86 us (1%)
    all_to_all x1, blocking collectives, local(): lax.all_to_all(values, 'head', split_axis=1, concat_axis=0, tiled=True)  57.3 us
    all_to_all x1, blocking collectives, local(): lax.all_to_all(keys, 'head', split_axis=1, concat_axis=0, tiled=True)  51.9 us
    reshape x4, local copies, waits for them, and re-layouts, unit_block(): value_tiles[tile_ids].reshape(block_units, slot_count * TILE, heads_dev, DH)  50.3 us
    reshape x4, local copies, waits for them, and re-layouts, unit_block(): key_tiles[tile_ids].reshape(block_units, slot_count * TILE, heads_dev, DH)  50.3 us
    dot_general x4, matrix products, unit_block(): jnp.einsum('bqhd,bkhd->bhqk', query_block, key_block, preferred_element_t...  45.9 us
    dot_general x4, matrix products, unit_block(): jnp.einsum('bhqk,bkhd->bqhd', weight, value_block, preferred_element_type...  43 us
    gather x4, local copies, waits for them, and re-layouts, unit_block(): key_tiles[tile_ids].reshape(block_units, slot_count * TILE, heads_dev, DH)  35 us
    gather x4, local copies, waits for them, and re-layouts, unit_block(): value_tiles[tile_ids].reshape(block_units, slot_count * TILE, heads_dev, DH)  34.9 us
  transfers between devices with their start and end apart: 3, of which 1 were waited for; matrix products, arithmetic and copies ran while one was open for 2% of the time, Pallas kernels for 0%

commit v1 on v0

--- a/solution.py
+++ b/solution.py
@@ -1,17 +1,21 @@
+import functools
 import math
 
 import jax
 import jax.numpy as jnp
 from jax import lax
+from jax.experimental import pallas as pl
+from jax.experimental.pallas import tpu as pltpu
 from jax.sharding import PartitionSpec as P
 
 HEADS = 32
 DH = 128
 TILE = 128
 KTOK_DEV = 256
-
-
-def local(queries, keys, values, tile_list):
+EXP2_SCALE = math.log2(math.e) / math.sqrt(DH)
+
+
+def general_plan(queries, keys, values, tile_list):
     n_head = lax.axis_size("head")
     heads_dev = HEADS // n_head
     kv_index = lax.axis_index("kv")
@@ -77,6 +81,113 @@
     return regrouped.reshape(-1, HEADS * DH)
 
 
+def fold_rows(block, op):
+    return op(block.reshape(TILE // 8, 8, TILE), axis=0)
+
+
+def score_pass(lists, q_ref, k_ref, s_next, a_next, n_sel, extra=None):
+    query = q_ref[a_next]
+    peak = None
+    for j in range(n_sel):
+        key = k_ref[lists[a_next, j]]
+        s = lax.dot_general(key, query, (((1,), (1,)), ((), ())), preferred_element_type=jnp.float32)
+        s_next[j * TILE : (j + 1) * TILE, :] = s
+        part = fold_rows(s, jnp.max)
+        peak = part if peak is None else jnp.maximum(peak, part)
+        if extra is not None:
+            extra(j)
+    return jnp.max(peak, axis=0, keepdims=True)
+
+
+def weights_phase(lists, q_ref, k_ref, p_ref, l_ref, s_a, s_b, n_q, n_sel):
+    def both(a_next, s_next, a_now, s_now, peak):
+        sums = []
+
+        def weigh(j):
+            rows = slice(j * TILE, (j + 1) * TILE)
+            expo = jnp.exp2((s_now[rows, :] - peak) * EXP2_SCALE)
+            p_ref[a_now, rows, :] = expo.astype(jnp.bfloat16)
+            part = fold_rows(expo, jnp.sum)
+            sums[:] = [part if not sums else sums[0] + part]
+
+        peak_next = score_pass(lists, q_ref, k_ref, s_next, a_next, n_sel, weigh)
+        total = jnp.sum(sums[0], axis=0, keepdims=True)
+        l_ref[a_now] = jnp.broadcast_to(total, (8, TILE))
+        return peak_next
+
+    def pair(i, peak):
+        first = 2 * i
+        peak = both(first + 1, s_b, first, s_a, peak)
+        return both(jnp.minimum(first + 2, n_q - 1), s_a, first + 1, s_b, peak)
+
+    lax.fori_loop(0, n_q // 2, pair, score_pass(lists, q_ref, k_ref, s_a, 0, n_sel))
+
+
+def turn_values(v_ref, vt_ref):
+    def one(t, carry):
+        vt_ref[t] = v_ref[t].T
+        return carry
+
+    lax.fori_loop(0, v_ref.shape[0], one, 0)
+
+
+def output_tile(lists, vt_ref, p_ref, l_ref, a, n_sel):
+    group = math.gcd(n_sel, 8)
+    numer = jnp.zeros((DH, TILE), jnp.float32)
+    for g in range(0, n_sel, group):
+        value = jnp.concatenate([vt_ref[lists[a, g + j]] for j in range(group)], axis=1)
+        weight = p_ref[a, g * TILE : (g + group) * TILE, :]
+        numer += jnp.dot(value, weight, preferred_element_type=jnp.float32)
+    return (numer / l_ref[a][:1, :]).T.astype(jnp.bfloat16)
+
+
+def attend_kernel(lists, q_ref, k_ref, v_ref, o_ref, vt_ref, p_ref, l_ref, s_a, s_b):
+    n_q, n_sel = lists.shape
+    weights_phase(lists, q_ref, k_ref, p_ref, l_ref, s_a, s_b, n_q, n_sel)
+    turn_values(v_ref, vt_ref)
+
+    def one(a, carry):
+        o_ref[a] = output_tile(lists, vt_ref, p_ref, l_ref, a, n_sel)
+        return carry
+
+    lax.fori_loop(0, n_q, one, 0)
+
+
+def head_plan(queries, keys, values, tile_list):
+    n_q, n_sel = tile_list.shape
+    both = ("head", "kv")
+    own_rows = lax.dynamic_slice_in_dim(queries, lax.axis_index("kv") * TILE, TILE, 0)
+    query = lax.all_to_all(own_rows, both, split_axis=1, concat_axis=0, tiled=True)
+    key = lax.all_to_all(keys, both, split_axis=1, concat_axis=0, tiled=True)
+    value = lax.all_to_all(values, both, split_axis=1, concat_axis=0, tiled=True)
+    query, key, value = (x.reshape(-1, TILE, DH) for x in (query, key, value))
+    vmem = pl.BlockSpec(memory_space=pltpu.VMEM)
+    out = pl.pallas_call(
+        attend_kernel,
+        out_shape=jax.ShapeDtypeStruct((n_q, TILE, DH), jnp.bfloat16),
+        in_specs=[pl.BlockSpec(memory_space=pltpu.SMEM), vmem, vmem, vmem],
+        out_specs=vmem,
+        scratch_shapes=[
+            pltpu.VMEM(value.shape, jnp.bfloat16),
+            pltpu.VMEM((n_q, n_sel * TILE, TILE), jnp.bfloat16),
+            pltpu.VMEM((n_q, 8, TILE), jnp.float32),
+            pltpu.VMEM((n_sel * TILE, TILE), jnp.float32),
+            pltpu.VMEM((n_sel * TILE, TILE), jnp.float32),
+        ],
+        compiler_params=pltpu.CompilerParams(vmem_limit_bytes=56 * 2**20),
+    )(tile_list, query, key, value)
+    return lax.all_to_all(out.reshape(n_q * TILE, DH), both, split_axis=0, concat_axis=1, tiled=True)
+
+
+def local(queries, keys, values, tile_list):
+    n_kv = lax.axis_size("kv")
+    n_dev = lax.axis_size("head") * n_kv
+    one_each = HEADS == n_dev and queries.shape[0] == n_kv * TILE and tile_list.shape[0] == n_dev
+    if one_each and n_dev % 2 == 0 and keys.shape[0] % TILE == 0:
+        return head_plan(queries, keys, values, tile_list)
+    return general_plan(queries, keys, values, tile_list)
+
+
 def solution(mesh):
     return jax.shard_map(
         local,

time: 513 us -> 233 us (0.45)
  local copies, waits for them, and re-layouts: 200 us -> 14 us
  matrix products: 88.9 us -> 0 us
  blocking collectives: 140 us -> 82.8 us
  Pallas kernels: 0 us -> 55.1 us
  waiting for transfers between devices: 22.8 us -> 69.7 us
  other arithmetic: 34.8 us -> 0 us
  between operations: 13.5 us -> 0.03 us
  starting transfers between devices: 3.93 us -> 11 us
  loops' own time: 5.86 us -> 0 us
    reshape x13 -> x0, local copies, waits for them, and re-layouts: 103 us -> none  [the longest x4 50.3 us: unit_block(): value_tiles[tile_ids].reshape(block_units, slot_count * TILE, heads_dev, DH)]
    dot_general x8 -> x0, matrix products: 88.9 us -> none  [the longest x4 45.9 us: unit_block(): jnp.einsum('bqhd,bkhd->bhqk', query_block, key_block, preferred_element_t...]
    gather x8 -> x0, local copies, waits for them, and re-layouts: 69.9 us -> none  [the longest x4 35 us: unit_block(): key_tiles[tile_ids].reshape(block_units, slot_count * TILE, heads_dev, DH)]
    all_to_all x3 -> x2, blocking collectives: 140 us -> 82.8 us  [the longest x1 52.8 us: head_plan(): lax.all_to_all(values, both, split_axis=1, concat_axis=0, tiled=True)]
    pallas_call x0 -> x1, Pallas kernels: none -> 55.1 us  [head_plan(): pl.pallas_call(attend_kernel, out_shape=jax.ShapeDtypeStruct((n_q, TILE,...]
    all_to_all x1 -> x2, waiting for transfers between devices: 22.7 us -> 69.7 us  [the longest x1 45.4 us: head_plan(): key = lax.all_to_all(keys, both, split_axis=1, concat_axis=0, tiled=True)]
    reduce_sum x5 -> x0, other arithmetic: 34.6 us -> none  [the longest x4 34.5 us: unit_block(): row_total = jnp.sum(exponent, axis=-1)]
    unnamed x9 -> x5, local copies, waits for them, and re-layouts: 9.62 us -> 1.32 us
  transfers between devices with their start and end apart: 3 -> 2, of which waited for: 1 -> 2; matrix products, arithmetic and copies ran while one was open for 2% -> 2% of each run, Pallas kernels for 0% -> 0%
where the time goes in v1:
time: 233 us
  blocking collectives  82.8 us (36%)
  waiting for transfers between devices  69.7 us (30%)
  Pallas kernels  55.1 us (24%)
  local copies, waits for them, and re-layouts  14 us (6%)
  starting transfers between devices  11 us (5%)
    pallas_call x1, Pallas kernels, head_plan(): pl.pallas_call(attend_kernel, out_shape=jax.ShapeDtypeStruct((n_q, TILE,...  55.1 us
    all_to_all x1, blocking collectives, head_plan(): lax.all_to_all(values, both, split_axis=1, concat_axis=0, tiled=True)  52.8 us
    all_to_all x1, waiting for transfers between devices, head_plan(): key = lax.all_to_all(keys, both, split_axis=1, concat_axis=0, tiled=True)  45.4 us
    all_to_all x1, blocking collectives, head_plan(): lax.all_to_all(out.reshape(n_q * TILE, DH), both, split_axis=0, concat_ax...  29.9 us
    all_to_all x1, waiting for transfers between devices, head_plan(): lax.all_to_all(own_rows, both, split_axis=1, concat_axis=0, tiled=True)  24.3 us
    all_to_all x1, starting transfers between devices, head_plan(): lax.all_to_all(own_rows, both, split_axis=1, concat_axis=0, tiled=True)  7.3 us
  transfers between devices with their start and end apart: 2, of which 2 were waited for; matrix products, arithmetic and copies ran while one was open for 2% of the time, Pallas kernels for 0%

profile of v1, /device:TPU:0, one launch (start us, length us, event | category | flops | bytes accessed | tf_op | source)
XLA Modules:
  0.0 232.6 jit_solution(16294331609636716874)
XLA Ops:
  0.0 0.0 copy-start
  0.0 1.4 constant_dynamic-slice_fusion
  1.4 1.3 copy.13
  2.8 2.3 copy.8
  5.0 7.3 %all-to-all-start = ((bf16[128,32,128]{2,0,1:T(8,128)(2,1)}), bf16[128,32,128]{2,0,1:T(8,128)(2,1)S(1)}, u32[]{:S(2)}, u32[]{:S(2)}) async-start(bf16[128,32,128]{2,0,1:T(8,128)(2,1)} %copy.8), calls=%async_computation | async-start | bytes 2097152 | tf_op jit(solution)/shard_map/all_to_all | solution.py:160
  12.3 0.0 copy-done
  12.3 1.9 copy_bitcast_fusion.1
  14.2 24.3 %all-to-all-done = bf16[128,32,128]{2,0,1:T(8,128)(2,1)S(1)} async-done(((bf16[128,32,128]{2,0,1:T(8,128)(2,1)}), bf16[128,32,128]{2,0,1:T(8,128)(2,1)S(1)}, u32[]{:S(2)}, u32[]{:S(2)}) %all-to-all-start) | async-done | bytes 1048608 | tf_op jit(solution)/shard_map/all_to_all | solution.py:160
  38.6 0.0 copy-start.1
  38.6 3.7 %all-to-all-start.1 = ((bf16[256,32,128]{2,0,1:T(8,128)(2,1)}), bf16[256,32,128]{2,0,1:T(8,128)(2,1)}, u32[]{:S(2)}, u32[]{:S(2)}) async-start(bf16[256,32,128]{2,0,1:T(8,128)(2,1)} %copy_bitcast_fusion.1), calls=%async_computation.1 | async-start | bytes 4194304 | tf_op jit(solution)/shard_map/all_to_all | solution.py:161
  42.3 3.5 %copy_bitcast_fusion = bf16[256,32,128]{2,0,1:T(8,128)(2,1)} fusion(bf16[256,4096]{1,0:T(8,128)(2,1)} %param.6), kind=kLoop, calls=%fused_computation | loop fusion | bytes 4194304 | tf_op jit(solution)/shard_map/all_to_all | solution.py:162
  45.8 0.0 copy-done.1
  45.8 45.4 %all-to-all-done.1 = bf16[256,32,128]{2,0,1:T(8,128)(2,1)} async-done(((bf16[256,32,128]{2,0,1:T(8,128)(2,1)}), bf16[256,32,128]{2,0,1:T(8,128)(2,1)}, u32[]{:S(2)}, u32[]{:S(2)}) %all-to-all-start.1) | async-done | bytes 2097184 | tf_op jit(solution)/shard_map/all_to_all | solution.py:161
  91.2 52.8 %all_to_all.64 = bf16[256,32,128]{2,0,1:T(8,128)(2,1)} all-to-all(bf16[256,32,128]{2,0,1:T(8,128)(2,1)} %copy_bitcast_fusion), channel_id=1, replica_groups=mesh['clip'=1,'head'=16,'kv'=2] {'head','kv'}, dimensions={1} | all-to-all | bytes 4194304 | tf_op jit(solution)/shard_map/all_to_all | solution.py:162
  144.0 55.1 %shard_map.46 = bf16[32,128,128]{2,1,0:T(8,128)(2,1)} custom-call(s32[32,32]{1,0:T(8,128)} %lists.1, bf16[32,128,128]{2,1,0:T(8,128)(2,1)} %bitcast.24, bf16[64,128,128]{2,1,0:T(8,128)(2,1)} %bitcast.3.k_ref, bf16[64,128,128]{2,1,0:T(8,128)(2,1)} %bitcast.20), custom_call_target="tpu_custom_call" | custom-call | tf_op jit(solution)/shard_map/pallas_call | solution.py:165
  199.1 29.9 %all_to_all.65 = bf16[32,128,128]{2,1,0:T(8,128)(2,1)S(1)} all-to-all(bf16[32,128,128]{2,1,0:T(8,128)(2,1)} %shard_map.46), channel_id=1, replica_groups=mesh['clip'=1,'head'=16,'kv'=2] {'head','kv'}, dimensions={0} | all-to-all | bytes 2097152 | tf_op jit(solution)/shard_map/all_to_all | solution.py:179
  229.0 1.3 copy.11
  230.3 2.3 copy.12
Async XLA Ops:
  0.0 12.3 %copy-start = (bf16[256,4096]{1,0:T(8,128)(2,1)S(1)}, bf16[256,4096]{1,0:T(8,128)(2,1)}, u32[]{:S(2)}) copy-start(bf16[256,4096]{1,0:T(8,128)(2,1)} %param.5) | copy-start | bytes 6291460
  5.0 33.5 %all-to-all-start = ((bf16[128,32,128]{2,0,1:T(8,128)(2,1)}), bf16[128,32,128]{2,0,1:T(8,128)(2,1)S(1)}, u32[]{:S(2)}, u32[]{:S(2)}) async-start(bf16[128,32,128]{2,0,1:T(8,128)(2,1)} %copy.8), calls=%async_computation | async-start | bytes 2097152 | tf_op jit(solution)/shard_map/all_to_all | solution.py:160
  38.6 7.3 %copy-start.1 = (bf16[128,32,128]{2,0,1:T(8,128)(2,1)}, bf16[128,32,128]{2,0,1:T(8,128)(2,1)S(1)}, u32[]{:S(2)}) copy-start(bf16[128,32,128]{2,0,1:T(8,128)(2,1)S(1)} %all-to-all-done) | copy-start | bytes 3145732
  38.6 52.6 %all-to-all-start.1 = ((bf16[256,32,128]{2,0,1:T(8,128)(2,1)}), bf16[256,32,128]{2,0,1:T(8,128)(2,1)}, u32[]{:S(2)}, u32[]{:S(2)}) async-start(bf16[256,32,128]{2,0,1:T(8,128)(2,1)} %copy_bitcast_fusion.1), calls=%async_computation.1 | async-start | bytes 4194304 | tf_op jit(solution)/shard_map/all_to_all | solution.py:161

commit v2 on v1

--- a/solution.py
+++ b/solution.py
@@ -141,42 +141,136 @@
     return (numer / l_ref[a][:1, :]).T.astype(jnp.bfloat16)
 
 
-def attend_kernel(lists, q_ref, k_ref, v_ref, o_ref, vt_ref, p_ref, l_ref, s_a, s_b):
+def fused_kernel(
+    lists, q_hbm, k_hbm, v_hbm, o_hbm, q_ref, k_ref, v_ref, vt_ref, p_ref, l_ref, s_a, s_b, stage, send, recv, own
+):
     n_q, n_sel = lists.shape
+    n_kv = lax.axis_size("kv")
+    n_dev = lax.axis_size("head") * n_kv
+    kv = lax.axis_index("kv")
+    me = lax.axis_index("head") * n_kv + kv
+    per_dev = k_hbm.shape[0]
+
+    def where(p):
+        return {"head": p // n_kv, "kv": lax.rem(p, n_kv)}
+
+    def columns(p):
+        return pl.ds(pl.multiple_of(p * DH, DH), DH)
+
+    barrier = pltpu.get_barrier_semaphore()
+
+    def greet(i, carry):
+        pl.semaphore_signal(
+            barrier, inc=1, device_id=where(lax.rem(me + i, n_dev)), device_id_type=pl.DeviceIdType.MESH
+        )
+        return carry
+
+    lax.fori_loop(1, n_dev, greet, 0)
+    pl.semaphore_wait(barrier, n_dev - 1)
+
+    def blocks(p):
+        token = pl.ds(me * per_dev, per_dev)
+        return (
+            (q_hbm.at[pl.ds(kv, 1), :, columns(p)], q_ref.at[pl.ds(me, 1)]),
+            (k_hbm.at[:, :, columns(p)], k_ref.at[token]),
+            (v_hbm.at[:, :, columns(p)], v_ref.at[token]),
+        )
+
+    mine = [pltpu.make_async_copy(src, dst, own.at[c]) for c, (src, dst) in enumerate(blocks(me))]
+    for copy in mine:
+        copy.start()
+
+    def push(kinds):
+        def one(i, carry):
+            p = lax.rem(me + i, n_dev)
+            pairs = blocks(p)
+            for c in kinds:
+                pltpu.make_async_remote_copy(
+                    src_ref=pairs[c][0],
+                    dst_ref=pairs[c][1],
+                    send_sem=send.at[c],
+                    recv_sem=recv.at[c],
+                    device_id=where(p),
+                    device_id_type=pl.DeviceIdType.MESH,
+                ).start()
+            return carry
+
+        lax.fori_loop(1, n_dev, one, 0)
+
+    def take(buffer, count, sem):
+        span = buffer.at[pl.ds(0, (n_dev - 1) * count)]
+        pltpu.make_async_copy(span, span, sem).wait()
+
+    push((0, 1))
+    push((2,))
+    take(q_ref, 1, recv.at[0])
+    take(k_ref, per_dev, recv.at[1])
+    mine[0].wait()
+    mine[1].wait()
     weights_phase(lists, q_ref, k_ref, p_ref, l_ref, s_a, s_b, n_q, n_sel)
+    take(v_ref, per_dev, recv.at[2])
+    mine[2].wait()
     turn_values(v_ref, vt_ref)
 
-    def one(a, carry):
-        o_ref[a] = output_tile(lists, vt_ref, p_ref, l_ref, a, n_sel)
+    def one(i, carry):
+        a = lax.rem(me + i, n_dev)
+        stage[a] = output_tile(lists, vt_ref, p_ref, l_ref, a, n_sel)
+
+        @pl.when(i < n_dev)
+        def _():
+            pltpu.make_async_remote_copy(
+                src_ref=stage.at[a],
+                dst_ref=o_hbm.at[:, columns(me)],
+                send_sem=send.at[3],
+                recv_sem=recv.at[3],
+                device_id=where(a),
+                device_id_type=pl.DeviceIdType.MESH,
+            ).start()
+
         return carry
 
-    lax.fori_loop(0, n_q, one, 0)
+    lax.fori_loop(1, n_dev + 1, one, 0)
+    last = pltpu.make_async_copy(stage.at[me], o_hbm.at[:, columns(me)], own.at[3])
+    last.start()
+    take(q_ref, 1, send.at[0])
+    take(k_ref, per_dev, send.at[1])
+    take(v_ref, per_dev, send.at[2])
+    take(stage, 1, send.at[3])
+    take(stage, 1, recv.at[3])
+    last.wait()
 
 
 def head_plan(queries, keys, values, tile_list):
     n_q, n_sel = tile_list.shape
-    both = ("head", "kv")
-    own_rows = lax.dynamic_slice_in_dim(queries, lax.axis_index("kv") * TILE, TILE, 0)
-    query = lax.all_to_all(own_rows, both, split_axis=1, concat_axis=0, tiled=True)
-    key = lax.all_to_all(keys, both, split_axis=1, concat_axis=0, tiled=True)
-    value = lax.all_to_all(values, both, split_axis=1, concat_axis=0, tiled=True)
-    query, key, value = (x.reshape(-1, TILE, DH) for x in (query, key, value))
-    vmem = pl.BlockSpec(memory_space=pltpu.VMEM)
-    out = pl.pallas_call(
-        attend_kernel,
-        out_shape=jax.ShapeDtypeStruct((n_q, TILE, DH), jnp.bfloat16),
-        in_specs=[pl.BlockSpec(memory_space=pltpu.SMEM), vmem, vmem, vmem],
-        out_specs=vmem,
+    n_dev = lax.axis_size("head") * lax.axis_size("kv")
+    queries, keys, values = (x.reshape(-1, TILE, HEADS * DH) for x in (queries, keys, values))
+    k_tiles = n_dev * keys.shape[0]
+    hbm = pl.BlockSpec(memory_space=pl.ANY)
+    flops = 4 * n_q * n_sel * TILE * TILE * DH
+    return pl.pallas_call(
+        fused_kernel,
+        out_shape=jax.ShapeDtypeStruct((TILE, HEADS * DH), jnp.bfloat16),
+        in_specs=[pl.BlockSpec(memory_space=pltpu.SMEM), hbm, hbm, hbm],
+        out_specs=hbm,
         scratch_shapes=[
-            pltpu.VMEM(value.shape, jnp.bfloat16),
+            pltpu.VMEM((n_q, TILE, DH), jnp.bfloat16),
+            pltpu.VMEM((k_tiles, TILE, DH), jnp.bfloat16),
+            pltpu.VMEM((k_tiles, TILE, DH), jnp.bfloat16),
+            pltpu.VMEM((k_tiles, DH, TILE), jnp.bfloat16),
             pltpu.VMEM((n_q, n_sel * TILE, TILE), jnp.bfloat16),
             pltpu.VMEM((n_q, 8, TILE), jnp.float32),
             pltpu.VMEM((n_sel * TILE, TILE), jnp.float32),
             pltpu.VMEM((n_sel * TILE, TILE), jnp.float32),
+            pltpu.VMEM((n_q, TILE, DH), jnp.bfloat16),
+            pltpu.SemaphoreType.DMA((4,)),
+            pltpu.SemaphoreType.DMA((4,)),
+            pltpu.SemaphoreType.DMA((4,)),
         ],
-        compiler_params=pltpu.CompilerParams(vmem_limit_bytes=56 * 2**20),
-    )(tile_list, query, key, value)
-    return lax.all_to_all(out.reshape(n_q * TILE, DH), both, split_axis=0, concat_axis=1, tiled=True)
+        compiler_params=pltpu.CompilerParams(
+            collective_id=0, has_side_effects=True, vmem_limit_bytes=56 * 2**20
+        ),
+        cost_estimate=pl.CostEstimate(flops=flops, bytes_accessed=8 * keys.size, transcendentals=0),
+    )(tile_list, queries, keys, values)
 
 
 def local(queries, keys, values, tile_list):

time: 233 us -> 167 us (0.72)
  the two profiles are of different devices: /device:TPU:0 before, /device:TPU:23 now
where the time goes in v2:
time: 167 us
  Pallas kernels  164 us (98%)
  local copies, waits for them, and re-layouts  2.29 us (1%)
    pallas_call x1, Pallas kernels, head_plan(): pl.pallas_call(fused_kernel, out_shape=jax.ShapeDtypeStruct((TILE, HEADS...  164 us

profile of v2, /device:TPU:23, one launch (start us, length us, event | category | flops | bytes accessed | tf_op | source)
XLA Modules:
  0.0 166.7 jit_solution(16818242847002989263)
XLA Ops:
  0.0 164.4 %shard_map.46 = bf16[128,4096]{1,0:T(8,128)(2,1)} custom-call(s32[32,32]{1,0:T(8,128)} %lists.1, bf16[2,128,4096]{2,1,0:T(8,128)(2,1)} %bitcast.3, bf16[2,128,4096]{2,1,0:T(8,128)(2,1)} %bitcast.4, bf16[2,128,4096]{2,1,0:T(8,128)(2,1)} %bitcast.5), custom_call_target="tpu_custom_call" | custom-call | flops 8589934592 | bytes 8388608 | tf_op jit(solution)/shard_map/pallas_call | solution.py:250
  164.4 2.3 %copy.6 = bf16[128,4096]{1,0:T(8,128)(2,1)} copy(bf16[128,4096]{1,0:T(8,128)(2,1)} %shard_map.46) | data formatting | bytes 2097152

commit v3 on v2

--- a/solution.py
+++ b/solution.py
@@ -123,14 +123,6 @@
     lax.fori_loop(0, n_q // 2, pair, score_pass(lists, q_ref, k_ref, s_a, 0, n_sel))
 
 
-def turn_values(v_ref, vt_ref):
-    def one(t, carry):
-        vt_ref[t] = v_ref[t].T
-        return carry
-
-    lax.fori_loop(0, v_ref.shape[0], one, 0)
-
-
 def output_tile(lists, vt_ref, p_ref, l_ref, a, n_sel):
     group = math.gcd(n_sel, 8)
     numer = jnp.zeros((DH, TILE), jnp.float32)
@@ -142,7 +134,7 @@
 
 
 def fused_kernel(
-    lists, q_hbm, k_hbm, v_hbm, o_hbm, q_ref, k_ref, v_ref, vt_ref, p_ref, l_ref, s_a, s_b, stage, send, recv, own
+    lists, q_hbm, k_hbm, v_hbm, o_hbm, q_ref, k_ref, v_raw, vt_out, vt_ref, p_ref, l_ref, s_a, s_b, stage, send, recv, own
 ):
     n_q, n_sel = lists.shape
     n_kv = lax.axis_size("kv")
@@ -157,6 +149,11 @@
     def columns(p):
         return pl.ds(pl.multiple_of(p * DH, DH), DH)
 
+    def partner(i):
+        return lax.rem(me + i // 2 + i % 2 * (n_dev // 2), n_dev)
+
+    load_values = pltpu.make_async_copy(v_hbm, v_raw, own.at[4])
+    load_values.start()
     barrier = pltpu.get_barrier_semaphore()
 
     def greet(i, carry):
@@ -168,21 +165,20 @@
     lax.fori_loop(1, n_dev, greet, 0)
     pl.semaphore_wait(barrier, n_dev - 1)
 
+    token = pl.ds(me * per_dev, per_dev)
+
     def blocks(p):
-        token = pl.ds(me * per_dev, per_dev)
         return (
             (q_hbm.at[pl.ds(kv, 1), :, columns(p)], q_ref.at[pl.ds(me, 1)]),
             (k_hbm.at[:, :, columns(p)], k_ref.at[token]),
-            (v_hbm.at[:, :, columns(p)], v_ref.at[token]),
+            (vt_out.at[p], vt_ref.at[token]),
         )
 
     mine = [pltpu.make_async_copy(src, dst, own.at[c]) for c, (src, dst) in enumerate(blocks(me))]
-    for copy in mine:
-        copy.start()
 
     def push(kinds):
         def one(i, carry):
-            p = lax.rem(me + i, n_dev)
+            p = partner(i)
             pairs = blocks(p)
             for c in kinds:
                 pltpu.make_async_remote_copy(
@@ -202,39 +198,46 @@
         pltpu.make_async_copy(span, span, sem).wait()
 
     push((0, 1))
+    mine[0].start()
+    mine[1].start()
+    load_values.wait()
+
+    def turn(p, carry):
+        for b in range(per_dev):
+            vt_out[p, b] = v_raw[b, :, columns(p)].T
+        return carry
+
+    lax.fori_loop(0, n_dev, turn, 0)
+    mine[2].start()
+    take(q_ref, 1, send.at[0])
+    take(k_ref, per_dev, send.at[1])
     push((2,))
     take(q_ref, 1, recv.at[0])
     take(k_ref, per_dev, recv.at[1])
     mine[0].wait()
     mine[1].wait()
     weights_phase(lists, q_ref, k_ref, p_ref, l_ref, s_a, s_b, n_q, n_sel)
-    take(v_ref, per_dev, recv.at[2])
+    take(vt_ref, per_dev, recv.at[2])
     mine[2].wait()
-    turn_values(v_ref, vt_ref)
 
     def one(i, carry):
-        a = lax.rem(me + i, n_dev)
+        a = partner(i)
         stage[a] = output_tile(lists, vt_ref, p_ref, l_ref, a, n_sel)
-
-        @pl.when(i < n_dev)
-        def _():
-            pltpu.make_async_remote_copy(
-                src_ref=stage.at[a],
-                dst_ref=o_hbm.at[:, columns(me)],
-                send_sem=send.at[3],
-                recv_sem=recv.at[3],
-                device_id=where(a),
-                device_id_type=pl.DeviceIdType.MESH,
-            ).start()
-
+        pltpu.make_async_remote_copy(
+            src_ref=stage.at[a],
+            dst_ref=o_hbm.at[:, columns(me)],
+            send_sem=send.at[3],
+            recv_sem=recv.at[3],
+            device_id=where(a),
+            device_id_type=pl.DeviceIdType.MESH,
+        ).start()
         return carry
 
-    lax.fori_loop(1, n_dev + 1, one, 0)
+    lax.fori_loop(1, n_dev, one, 0)
+    stage[me] = output_tile(lists, vt_ref, p_ref, l_ref, me, n_sel)
     last = pltpu.make_async_copy(stage.at[me], o_hbm.at[:, columns(me)], own.at[3])
     last.start()
-    take(q_ref, 1, send.at[0])
-    take(k_ref, per_dev, send.at[1])
-    take(v_ref, per_dev, send.at[2])
+    take(vt_ref, per_dev, send.at[2])
     take(stage, 1, send.at[3])
     take(stage, 1, recv.at[3])
     last.wait()
@@ -255,7 +258,8 @@
         scratch_shapes=[
             pltpu.VMEM((n_q, TILE, DH), jnp.bfloat16),
             pltpu.VMEM((k_tiles, TILE, DH), jnp.bfloat16),
-            pltpu.VMEM((k_tiles, TILE, DH), jnp.bfloat16),
+            pltpu.VMEM(values.shape, jnp.bfloat16),
+            pltpu.VMEM((n_dev, values.shape[0], DH, TILE), jnp.bfloat16),
             pltpu.VMEM((k_tiles, DH, TILE), jnp.bfloat16),
             pltpu.VMEM((n_q, n_sel * TILE, TILE), jnp.bfloat16),
             pltpu.VMEM((n_q, 8, TILE), jnp.float32),
@@ -264,7 +268,7 @@
             pltpu.VMEM((n_q, TILE, DH), jnp.bfloat16),
             pltpu.SemaphoreType.DMA((4,)),
             pltpu.SemaphoreType.DMA((4,)),
-            pltpu.SemaphoreType.DMA((4,)),
+            pltpu.SemaphoreType.DMA((5,)),
         ],
         compiler_params=pltpu.CompilerParams(
             collective_id=0, has_side_effects=True, vmem_limit_bytes=56 * 2**20

time: 167 us -> 161 us (0.964)
  the two profiles are of different devices: /device:TPU:23 before, /device:TPU:0 now
where the time goes in v3:
time: 161 us
  Pallas kernels  158 us (98%)
  local copies, waits for them, and re-layouts  2.29 us (1%)
    pallas_call x1, Pallas kernels, head_plan(): pl.pallas_call(fused_kernel, out_shape=jax.ShapeDtypeStruct((TILE, HEADS...  158 us

profile of v3, /device:TPU:0, one launch (start us, length us, event | category | flops | bytes accessed | tf_op | source)
XLA Modules:
  0.0 160.6 jit_solution(3213336097456338567)
XLA Ops:
  0.0 158.3 %shard_map.46 = bf16[128,4096]{1,0:T(8,128)(2,1)} custom-call(s32[32,32]{1,0:T(8,128)} %lists.1, bf16[2,128,4096]{2,1,0:T(8,128)(2,1)} %bitcast.3, bf16[2,128,4096]{2,1,0:T(8,128)(2,1)} %bitcast.4, bf16[2,128,4096]{2,1,0:T(8,128)(2,1)} %bitcast.5), custom_call_target="tpu_custom_call" | custom-call | flops 8589934592 | bytes 8388608 | tf_op jit(solution)/shard_map/pallas_call | solution.py:253
  158.3 2.3 %copy.6 = bf16[128,4096]{1,0:T(8,128)(2,1)} copy(bf16[128,4096]{1,0:T(8,128)(2,1)} %shard_map.46) | data formatting | bytes 2097152

commit v4 on v3

--- a/solution.py
+++ b/solution.py
@@ -134,7 +134,7 @@
 
 
 def fused_kernel(
-    lists, q_hbm, k_hbm, v_hbm, o_hbm, q_ref, k_ref, v_raw, vt_out, vt_ref, p_ref, l_ref, s_a, s_b, stage, send, recv, own
+    lists, q_hbm, k_hbm, v_hbm, o_hbm, q_ref, k_ref, q_out, k_out, v_raw, vt_out, vt_ref, p_ref, l_ref, s_a, s_b, stage, send, recv, own
 ):
     n_q, n_sel = lists.shape
     n_kv = lax.axis_size("kv")
@@ -152,6 +152,12 @@
     def partner(i):
         return lax.rem(me + i // 2 + i % 2 * (n_dev // 2), n_dev)
 
+    def load(p, carry):
+        pltpu.make_async_copy(q_hbm.at[kv, :, columns(p)], q_out.at[p], own.at[5]).start()
+        pltpu.make_async_copy(k_hbm.at[:, :, columns(p)], k_out.at[p], own.at[6]).start()
+        return carry
+
+    lax.fori_loop(0, n_dev, load, 0)
     load_values = pltpu.make_async_copy(v_hbm, v_raw, own.at[4])
     load_values.start()
     barrier = pltpu.get_barrier_semaphore()
@@ -169,14 +175,14 @@
 
     def blocks(p):
         return (
-            (q_hbm.at[pl.ds(kv, 1), :, columns(p)], q_ref.at[pl.ds(me, 1)]),
-            (k_hbm.at[:, :, columns(p)], k_ref.at[token]),
+            (q_out.at[p], q_ref.at[me]),
+            (k_out.at[p], k_ref.at[token]),
             (vt_out.at[p], vt_ref.at[token]),
         )
 
     mine = [pltpu.make_async_copy(src, dst, own.at[c]) for c, (src, dst) in enumerate(blocks(me))]
 
-    def push(kinds):
+    def push(kinds, first, end, k_send):
         def one(i, carry):
             p = partner(i)
             pairs = blocks(p)
@@ -184,20 +190,25 @@
                 pltpu.make_async_remote_copy(
                     src_ref=pairs[c][0],
                     dst_ref=pairs[c][1],
-                    send_sem=send.at[c],
+                    send_sem=send.at[k_send if c == 1 else c],
                     recv_sem=recv.at[c],
                     device_id=where(p),
                     device_id_type=pl.DeviceIdType.MESH,
                 ).start()
             return carry
 
-        lax.fori_loop(1, n_dev, one, 0)
+        lax.fori_loop(first, end, one, 0)
 
     def take(buffer, count, sem):
-        span = buffer.at[pl.ds(0, (n_dev - 1) * count)]
+        span = buffer.at[pl.ds(0, count)]
         pltpu.make_async_copy(span, span, sem).wait()
 
-    push((0, 1))
+    pltpu.make_async_copy(q_out, q_out, own.at[5]).wait()
+    pltpu.make_async_copy(k_out, k_out, own.at[6]).wait()
+    others = n_dev - 1
+    early = others * 2 // 3
+    push((0, 1), 1, early + 1, 1)
+    push((0, 1), early + 1, n_dev, 4)
     mine[0].start()
     mine[1].start()
     load_values.wait()
@@ -209,15 +220,14 @@
 
     lax.fori_loop(0, n_dev, turn, 0)
     mine[2].start()
-    take(q_ref, 1, send.at[0])
-    take(k_ref, per_dev, send.at[1])
-    push((2,))
-    take(q_ref, 1, recv.at[0])
-    take(k_ref, per_dev, recv.at[1])
+    take(k_ref, early * per_dev, send.at[1])
+    push((2,), 1, n_dev, 1)
+    take(q_ref, others, recv.at[0])
+    take(k_ref, others * per_dev, recv.at[1])
     mine[0].wait()
     mine[1].wait()
     weights_phase(lists, q_ref, k_ref, p_ref, l_ref, s_a, s_b, n_q, n_sel)
-    take(vt_ref, per_dev, recv.at[2])
+    take(vt_ref, others * per_dev, recv.at[2])
     mine[2].wait()
 
     def one(i, carry):
@@ -237,9 +247,11 @@
     stage[me] = output_tile(lists, vt_ref, p_ref, l_ref, me, n_sel)
     last = pltpu.make_async_copy(stage.at[me], o_hbm.at[:, columns(me)], own.at[3])
     last.start()
-    take(vt_ref, per_dev, send.at[2])
-    take(stage, 1, send.at[3])
-    take(stage, 1, recv.at[3])
+    take(q_ref, others, send.at[0])
+    take(k_ref, (others - early) * per_dev, send.at[4])
+    take(vt_ref, others * per_dev, send.at[2])
+    take(stage, others, send.at[3])
+    take(stage, others, recv.at[3])
     last.wait()
 
 
@@ -258,6 +270,8 @@
         scratch_shapes=[
             pltpu.VMEM((n_q, TILE, DH), jnp.bfloat16),
             pltpu.VMEM((k_tiles, TILE, DH), jnp.bfloat16),
+            pltpu.VMEM((n_dev, TILE, DH), jnp.bfloat16),
+            pltpu.VMEM((n_dev, keys.shape[0], TILE, DH), jnp.bfloat16),
             pltpu.VMEM(values.shape, jnp.bfloat16),
             pltpu.VMEM((n_dev, values.shape[0], DH, TILE), jnp.bfloat16),
             pltpu.VMEM((k_tiles, DH, TILE), jnp.bfloat16),
@@ -266,9 +280,9 @@
             pltpu.VMEM((n_sel * TILE, TILE), jnp.float32),
             pltpu.VMEM((n_sel * TILE, TILE), jnp.float32),
             pltpu.VMEM((n_q, TILE, DH), jnp.bfloat16),
+            pltpu.SemaphoreType.DMA((5,)),
             pltpu.SemaphoreType.DMA((4,)),
-            pltpu.SemaphoreType.DMA((4,)),
-            pltpu.SemaphoreType.DMA((5,)),
+            pltpu.SemaphoreType.DMA((7,)),
         ],
         compiler_params=pltpu.CompilerParams(
             collective_id=0, has_side_effects=True, vmem_limit_bytes=56 * 2**20

time: 161 us -> 158 us (0.981)
  Pallas kernels: 158 us -> 155 us
    pallas_call x1, Pallas kernels: 158 us -> 155 us  [head_plan(): pl.pallas_call(fused_kernel, out_shape=jax.ShapeDtypeStruct((TILE, HEADS...]
where the time goes in v4:
time: 158 us; the launch traced here: 157 us
  Pallas kernels  155 us (98%)
  local copies, waits for them, and re-layouts  2.29 us (1%)
    pallas_call x1, Pallas kernels, head_plan(): pl.pallas_call(fused_kernel, out_shape=jax.ShapeDtypeStruct((TILE, HEADS...  155 us

profile of v4, /device:TPU:0, one launch (start us, length us, event | category | flops | bytes accessed | tf_op | source)
XLA Modules:
  0.0 157.3 jit_solution(661193334750086409)
XLA Ops:
  0.0 155.0 %shard_map.46 = bf16[128,4096]{1,0:T(8,128)(2,1)} custom-call(s32[32,32]{1,0:T(8,128)} %lists.1, bf16[2,128,4096]{2,1,0:T(8,128)(2,1)} %bitcast.3, bf16[2,128,4096]{2,1,0:T(8,128)(2,1)} %bitcast.4, bf16[2,128,4096]{2,1,0:T(8,128)(2,1)} %bitcast.5), custom_call_target="tpu_custom_call" | custom-call | flops 8589934592 | bytes 8388608 | tf_op jit(solution)/shard_map/pallas_call | solution.py:265
  155.0 2.3 %copy.6 = bf16[128,4096]{1,0:T(8,128)(2,1)} copy(bf16[128,4096]{1,0:T(8,128)(2,1)} %shard_map.46) | data formatting | bytes 2097152

commit v5 on v4

--- a/solution.py
+++ b/solution.py
@@ -82,20 +82,22 @@
 
 
 def fold_rows(block, op):
-    return op(block.reshape(TILE // 8, 8, TILE), axis=0)
+    return op(block.reshape(-1, 8, TILE), axis=0)
 
 
 def score_pass(lists, q_ref, k_ref, s_next, a_next, n_sel, extra=None):
     query = q_ref[a_next]
     peak = None
-    for j in range(n_sel):
-        key = k_ref[lists[a_next, j]]
+    group = math.gcd(n_sel, 4)
+    for g in range(0, n_sel, group):
+        key = jnp.concatenate([k_ref[lists[a_next, g + j]] for j in range(group)], axis=0)
         s = lax.dot_general(key, query, (((1,), (1,)), ((), ())), preferred_element_type=jnp.float32)
-        s_next[j * TILE : (j + 1) * TILE, :] = s
+        s_next[g * TILE : (g + group) * TILE, :] = s
         part = fold_rows(s, jnp.max)
         peak = part if peak is None else jnp.maximum(peak, part)
         if extra is not None:
-            extra(j)
+            for j in range(group):
+                extra(g + j)
     return jnp.max(peak, axis=0, keepdims=True)
 
 

time: 158 us -> 152 us (0.962)
  Pallas kernels: 155 us -> 150 us
    pallas_call x1, Pallas kernels: 155 us -> 150 us  [head_plan(): pl.pallas_call(fused_kernel, out_shape=jax.ShapeDtypeStruct((TILE, HEADS...]
where the time goes in v5:
time: 152 us
  Pallas kernels  150 us (99%)
  local copies, waits for them, and re-layouts  2.29 us (2%)
    pallas_call x1, Pallas kernels, head_plan(): pl.pallas_call(fused_kernel, out_shape=jax.ShapeDtypeStruct((TILE, HEADS...  150 us

profile of v5, /device:TPU:0, one launch (start us, length us, event | category | flops | bytes accessed | tf_op | source)
XLA Modules:
  0.0 152.2 jit_solution(14973661187287408624)
XLA Ops:
  0.0 149.9 %shard_map.46 = bf16[128,4096]{1,0:T(8,128)(2,1)} custom-call(s32[32,32]{1,0:T(8,128)} %lists.1, bf16[2,128,4096]{2,1,0:T(8,128)(2,1)} %bitcast.3, bf16[2,128,4096]{2,1,0:T(8,128)(2,1)} %bitcast.4, bf16[2,128,4096]{2,1,0:T(8,128)(2,1)} %bitcast.5), custom_call_target="tpu_custom_call" | custom-call | flops 8589934592 | bytes 8388608 | tf_op jit(solution)/shard_map/pallas_call | solution.py:267
  149.9 2.3 %copy.6 = bf16[128,4096]{1,0:T(8,128)(2,1)} copy(bf16[128,4096]{1,0:T(8,128)(2,1)} %shard_map.46) | data formatting | bytes 2097152
